TPU v7x, 512 devices: a whole 4x8x8 slice. The times are simulated.
512 devices in a mesh: leaf: 4 (over z_hi), row: 8 (over y), col: 16 (over z_lo, x, core).
Axes of the slice: x: 4, y: 8, z: 8 (z_hi: 4, z_lo: 2; z = z_hi * 2 + z_lo), core: 2. Of those that a mesh axis runs over, the one named last changes fastest.
Arguments:
- y_root: bfloat16 [16384, 256], P('col', ('leaf', 'row')), may hold values from -6 to 6
- root_inverse: bfloat16 [16384, 16384], P(('leaf', 'row'), 'col'), may hold values from -0.046875 to 0.046875
- block_map: int32 [4, 16], replicated, may hold values from 0 to 63, as said below
- y_child: bfloat16 [4, 12288, 256], P('leaf', 'row'), may hold values from -6 to 6
- panel: bfloat16 [4, 12288, 4096], P('leaf', 'row', 'col'), may hold values from -0.09375 to 0.09375
- child_inverse: bfloat16 [4, 12288, 12288], P('leaf', 'row', 'col'), may hold values from -0.0546875 to 0.0546875
Outputs:
- x_root: bfloat16 [16384, 256], P(('leaf', 'row', 'col'))
- x_child: bfloat16 [4, 12288, 256], P('leaf', ('row', 'col'))
Inputs may be any that keep to these rules, and one draw needn't show every extreme that they name: `block_map`: each of the 16384 // 256 root blocks appears exactly once in the whole map; the blocks of child k are all those of root rows g * 4096 to (g + 1) * 4096 - 1 for one group g, which is k or (k + 2) % 4, in an order drawn from the seed.
All inputs are finite; a program needn't handle non-finite values.
Results may differ from a plain program's by a relative error of at most 0.018.
Values may be sent and summed in bfloat16 or wider, within the bound.
A program may use at most 64 MiB of HBM per device.

v0:
```python
import jax
import jax.numpy as jnp
from jax import lax
from jax.sharding import PartitionSpec as P

BLK = 256


def from_root(block, axis, source):
    block = jnp.where(lax.axis_index(axis) == source, block, jnp.zeros_like(block))
    return lax.psum(block, axis)


def per_device(y_root, root_inverse, block_map, y_child, panel, child_inverse):
    row_count = lax.axis_size("row")
    col_count = lax.axis_size("col")
    leaf_index = lax.axis_index("leaf")
    row_index = lax.axis_index("row")
    col_index = lax.axis_index("col")
    rhs_full = lax.all_gather(y_root, ("leaf", "row"), axis=1, tiled=True)
    panel_tile = panel[0]
    width_cols = panel_tile.shape[1]
    block_count = width_cols // BLK
    rhs_width = rhs_full.shape[1]
    child_map = lax.dynamic_index_in_dim(block_map, leaf_index, 0, keepdims=False)
    my_blocks = lax.dynamic_slice_in_dim(child_map, col_index * block_count, block_count)
    block_slots = jnp.arange(block_count, dtype=jnp.int32)
    zero_rows = jnp.zeros((width_cols, rhs_width), jnp.bfloat16)
    x_root = lax.psum_scatter(
        jnp.dot(root_inverse, rhs_full, preferred_element_type=jnp.float32),
        "col",
        scatter_dimension=0,
        tiled=True,
    ).astype(jnp.bfloat16)
    shard_rows = lax.all_gather(x_root, ("leaf", "row", "col"), axis=0, tiled=True)
    count_here = shard_rows.shape[0]
    global_rows = jnp.arange(count_here, dtype=jnp.int32)
    hits = (global_rows // BLK)[:, None] == my_blocks[None, :]
    found = jnp.any(hits, axis=1)
    slot = jnp.sum(jnp.where(hits, block_slots[None, :], 0), axis=1)
    target = jnp.where(found, slot * BLK + global_rows % BLK, zero_rows.shape[0])
    selected = zero_rows.at[target].set(shard_rows, mode="drop")
    inverse_tile = child_inverse[0]
    band_rows = y_child.shape[1]
    slab_rows = inverse_tile.shape[1]
    update = lax.psum(jnp.dot(panel_tile, selected, preferred_element_type=jnp.float32), "col")
    reduced = (y_child[0].astype(jnp.float32) - update).astype(jnp.bfloat16)
    owner_row = col_index * row_count // col_count
    offset = jnp.clip(col_index * slab_rows - row_index * band_rows, 0, band_rows - slab_rows)
    local_part = lax.dynamic_slice_in_dim(reduced, offset, slab_rows, 0)
    column_rhs = from_root(local_part, "row", owner_row)
    x_child = lax.psum_scatter(
        jnp.dot(inverse_tile, column_rhs, preferred_element_type=jnp.float32).astype(jnp.bfloat16),
        "col",
        scatter_dimension=0,
        tiled=True,
    )
    return (x_root, x_child[None])


def solution(mesh):
    in_specs = (
        P("col", ("leaf", "row")),
        P(("leaf", "row"), "col"),
        P(),
        P("leaf", "row", None),
        P("leaf", "row", "col"),
        P("leaf", "row", "col"),
    )
    out_specs = (P(("leaf", "row", "col"), None), P("leaf", ("row", "col"), None))
    return jax.shard_map(
        per_device, mesh=mesh, in_specs=in_specs, out_specs=out_specs, check_vma=False
    )
```

profile of v0, /device:TPU:1, one launch (start us, length us, event | category | flops | bytes accessed | tf_op | source)
XLA Modules:
  0.0 1338.5 jit_solution(15799035505042136396)
XLA Ops:
  7.2 0.0 copy-start
  7.2 0.0 copy-start.1
  7.2 0.0 reduce-scatter.5.cloned.1.call-start
  7.2 78.3 %all_gather.6 = bf16[1024,256]{0,1:T(8,128)(2,1)S(1)} all-gather(bf16[1024,8]{0,1:T(8,128)(2,1)} %param.6), channel_id=1, replica_groups=mesh['leaf'=4,'row'=8,'col'=16] {'leaf','row'}, dimensions={1}, use_global_device_ids=true | all-gather | bytes 540672 | tf_op jit(solution)/shard_map/all_gather | solution.py:20
  85.6 2.5 fusion.7
  88.1 0.0 reduce-scatter.5.cloned.1.call-update
  88.1 0.0 all-gather.2.cloned.1.call-start
  88.1 69.5 %reduce-scatter.5.cloned.1.call-done = f32[32,256]{1,0:T(8,128)} async-done(((f32[512,256]{1,0:T(8,128)}), f32[32,256]{1,0:T(8,128)}) %reduce-scatter.5.cloned.1.call-update) | async-done | bytes 32784 | tf_op jit(solution)/shard_map/reduce_scatter | solution.py:29
  157.6 1.4 convert_element_type.18
  159.0 0.0 all-gather.2.cloned.1.call-update
  159.0 0.0 all-reduce.3.cloned.1.call-start
  159.0 1.3 dynamic_slice.8
  160.3 0.8 compare_select_fusion
  161.1 815.3 %all-gather.2.cloned.1.call-done = bf16[16384,256]{1,0:T(8,128)(2,1)} async-done(((bf16[32,256]{1,0:T(8,128)(2,1)}), bf16[16384,256]{1,0:T(8,128)(2,1)}) %all-gather.2.cloned.1.call-update) | async-done | bytes 8388624 | tf_op jit(solution)/shard_map/all_gather | solution.py:35
  976.4 69.2 %scatter_custom_fusion = bf16[256,256]{1,0:T(8,128)(2,1)S(1)} fusion(s32[16384]{0:T(1024)S(1)} %bitcast.23, bf16[16384,256]{1,0:T(8,128)(2,1)} %all-gather.2.cloned.1.call-done, bf16[]{:T(256)} %constant.84.clone.1), kind=kCustom, calls=%fused_computation.16 | custom fusion | bytes 131584 | tf_op jit(solution)/shard_map/scatter | solution.py:42
  1045.6 0.0 copy-done.1
  1045.6 1.6 convolution_bitcast_fusion
  1047.2 0.0 all-reduce.3.cloned.1.call-update
  1047.2 0.0 all-reduce.5.cloned.1.call-start
  1047.3 1.4 copy.10
  1048.7 134.2 %all-reduce.3.cloned.1.call-done = f32[1536,256]{0,1:T(8,128)} async-done(((f32[1536,256]{0,1:T(8,128)}), f32[1536,256]{0,1:T(8,128)}) %all-reduce.3.cloned.1.call-update) | async-done | bytes 1572880 | tf_op jit(solution)/shard_map/psum | solution.py:46
  1182.8 2.3 fusion.4
  1185.2 0.0 all-reduce.5.cloned.1.call-update
  1185.2 0.0 reduce-scatter.7.cloned.1.call-start
  1185.2 74.7 %all-reduce.5.cloned.1.call-done = bf16[768,256]{0,1:T(8,128)(2,1)} async-done(((bf16[768,256]{0,1:T(8,128)(2,1)}), bf16[768,256]{0,1:T(8,128)(2,1)}) %all-reduce.5.cloned.1.call-update) | async-done | bytes 393232 | tf_op jit(solution)/shard_map/psum | solution.py:11
  1260.0 0.0 copy-done
  1260.0 1.8 fusion
  1261.8 1.2 copy.12
  1262.9 0.0 reduce-scatter.7.cloned.1.call-update
  1263.0 67.3 %reduce-scatter.7.cloned.1.call-done = bf16[96,256]{1,0:T(8,128)(2,1)} async-done(((bf16[1536,256]{1,0:T(8,128)(2,1)}), bf16[96,256]{1,0:T(8,128)(2,1)}) %reduce-scatter.7.cloned.1.call-update) | async-done | bytes 49168
  1330.3 0.9 copy.13
  1331.2 0.7 copy.11
Async XLA Ops:
  7.2 1252.8 %copy-start = (bf16[1,1536,768]{2,1,0:T(8,128)(2,1)S(1)}, bf16[1,1536,768]{2,1,0:T(8,128)(2,1)}, u32[]{:S(2)}) copy-start(bf16[1,1536,768]{2,1,0:T(8,128)(2,1)} %param.11) | copy-start | bytes 7077892
  7.2 1038.4 %copy-start.1 = (bf16[1,1536,256]{2,1,0:T(8,128)(2,1)S(1)}, bf16[1,1536,256]{2,1,0:T(8,128)(2,1)}, u32[]{:S(2)}) copy-start(bf16[1,1536,256]{2,1,0:T(8,128)(2,1)} %param.10) | copy-start | bytes 2359300
  7.2 150.4 %reduce-scatter.5.cloned.1.call-start = ((), (), s32[]{:S(2)}) async-start(), calls=%async_computation.2 | async-start | bytes 557056 | tf_op jit(solution)/shard_map/reduce_scatter | solution.py:29
  88.1 888.3 %all-gather.2.cloned.1.call-start = ((), (), s32[]{:S(2)}) async-start(), calls=%async_computation.3 | async-start | bytes 8404992 | tf_op jit(solution)/shard_map/all_gather | solution.py:35
  159.0 1023.9 %all-reduce.3.cloned.1.call-start = ((), (), s32[]{:S(2)}) async-start(), calls=%async_computation.4 | async-start | bytes 3145728 | tf_op jit(solution)/shard_map/psum | solution.py:46
  1047.2 212.8 %all-reduce.5.cloned.1.call-start = ((), (), s32[]{:S(2)}) async-start(), calls=%async_computation.5 | async-start | bytes 786432 | tf_op jit(solution)/shard_map/psum | solution.py:11
  1185.2 145.1 %reduce-scatter.7.cloned.1.call-start = ((), (), s32[]{:S(2)}) async-start(), calls=%async_computation.6 | async-start | bytes 835584
Sparse Core Ops, SparseCore 0:
  88.2 69.3 reduce-scatter.4
  160.6 815.7 all-gather.1
  1047.3 135.4 all-reduce.2
  1185.3 74.6 all-reduce.4
  1263.1 67.1 reduce-scatter.6
where the time goes:
time: 1340 us
  waiting for transfers between devices  1160 us (87%)
  blocking collectives  78.3 us (6%)
  local copies, waits for them, and re-layouts  74.6 us (6%)
  between operations  13.9 us (1%)
    all_gather x1, waiting for transfers between devices, per_device(): lax.all_gather(x_root, ('leaf', 'row', 'col'), axis=0, tiled=True)  815 us
    psum x1, waiting for transfers between devices, per_device(): lax.psum(jnp.dot(panel_tile, selected, preferred_element_type=jnp.float32...  134 us
    all_gather x1, blocking collectives, per_device(): rhs_full = lax.all_gather(y_root, ('leaf', 'row'), axis=1, tiled=True)  78.3 us
    psum x1, waiting for transfers between devices, from_root(): return lax.psum(block, axis)  74.7 us
    reduce_scatter x1, waiting for transfers between devices, per_device(): lax.psum_scatter(jnp.dot(root_inverse, rhs_full, preferred_element_type=j...  69.5 us
    scatter x1, local copies, waits for them, and re-layouts, per_device(): selected = zero_rows.at[target].set(shard_rows, mode='drop')  69.2 us
    unnamed x6, waiting for transfers between devices  67.4 us
  transfers between devices with their start and end apart: 5, of which 5 were waited for; matrix products, arithmetic and copies ran while one was open for 0% of the time, Pallas kernels for 0%

commit v1 on v0

v1 whole, which is shorter than its diff:
```python
import jax
import jax.numpy as jnp
from jax import lax
from jax.experimental import pallas as pl
from jax.experimental.pallas import tpu as pltpu
from jax.sharding import PartitionSpec as P

MESH = pl.DeviceIdType.MESH
BF, F32 = jnp.bfloat16, jnp.float32

LEAF, ROW, COL, CHIP = 4, 8, 16, 8
NH = 2
W = 256 // NH
LH = LEAF // NH

DMA = pltpu.SemaphoreType.DMA
SCRATCH = dict(
    inv_v=pltpu.VMEM((512, 1024), BF),
    panel_v=pltpu.VMEM((2, 768, 256), BF),
    cinv_v=pltpu.VMEM((2, 8, 96, 768), BF),
    yc_v=pltpu.VMEM((96, 256), BF),
    load=DMA((5,)),
    ybuf=pltpu.VMEM((LEAF, ROW, 16, 512), BF),
    z_s=DMA((3,)),
    z_r=DMA((3,)),
    ring_s=DMA((NH, 2, 4)),
    ring_r=DMA((NH, 2, 4)),
    xpart=pltpu.VMEM((NH, COL, 2, 16, W), BF),
    xin=pltpu.VMEM((NH, COL - 1, 2, 16, W), BF),
    xin_s=DMA((NH, COL - 1)),
    xin_r=DMA((NH, COL - 1)),
    **{f"xpair{h}": pltpu.VMEM((2, 2, 16, W), BF) for h in range(NH)},
    swap_s=DMA((NH,)),
    swap_r=DMA((NH,)),
    **{f"xg{h}": pltpu.VMEM((16, 16, W), BF) for h in range(NH)},
    xg_s=DMA((NH, ROW - 1)),
    xg_r=DMA((NH, ROW - 1)),
    picked=pltpu.VMEM((NH, COL - 1, 16, W), BF),
    sel=pltpu.VMEM((NH, COL, 16, W), BF),
    sel_s=DMA((NH, COL - 1)),
    sel_r=DMA((NH, COL - 1)),
    xo=pltpu.VMEM((2, NH, 16, W), BF),
    xo_s=DMA((NH, 2)),
    xo_r=DMA((NH, 2)),
    pother=pltpu.VMEM((NH, 8, 96, W), BF),
    pin=pltpu.VMEM((NH, 8, 96, W), BF),
    pin_s=DMA((NH,)),
    pin_r=DMA((NH,)),
    pown=pltpu.VMEM((NH, 8, 96, W), F32),
    pout=pltpu.VMEM((NH, CHIP - 1, 96, W), BF),
    prx=pltpu.VMEM((NH, CHIP - 1, 96, W), BF),
    prx_s=DMA((NH, CHIP - 1)),
    prx_r=DMA((NH, CHIP - 1)),
    red=pltpu.VMEM((NH, 96, W), BF),
    turn_s=DMA((NH,)),
    turn_r=DMA((NH,)),
    rf=pltpu.VMEM((NH, ROW, 96, W), BF),
    rf_s=DMA((NH, ROW - 1)),
    rf_r=DMA((NH, ROW - 1)),
    cother=pltpu.VMEM((NH, 8, 96, W), BF),
    cin=pltpu.VMEM((NH, 8, 96, W), BF),
    cin_s=DMA((NH,)),
    cin_r=DMA((NH,)),
    cown=pltpu.VMEM((NH, 8, 96, W), F32),
    cout=pltpu.VMEM((NH, CHIP - 1, 96, W), BF),
    crx=pltpu.VMEM((NH, CHIP - 1, 96, W), BF),
    crx_s=DMA((NH, CHIP - 1)),
    crx_r=DMA((NH, CHIP - 1)),
)


class Refs:
    pass


def kernel(y_ref, inv_ref, map_ref, yc_ref, panel_ref, cinv_ref, xroot_ref, xchild_ref, *scratch):
    k = Refs()
    for name, ref in zip(SCRATCH, scratch):
        setattr(k, name, ref)
    xpair = [getattr(k, f"xpair{h}") for h in range(NH)]
    xg = [getattr(k, f"xg{h}") for h in range(NH)]
    leaf, row, col = lax.axis_index("leaf"), lax.axis_index("row"), lax.axis_index("col")
    core, chip = col % 2, col // 2
    sent = []

    def remote(src, dst, send, recv, device):
        return pltpu.make_async_remote_copy(
            src_ref=src, dst_ref=dst, send_sem=send, recv_sem=recv, device_id=device, device_id_type=MESH
        )

    def go(copy):
        copy.start()
        sent.append(copy)

    def leaf_peer(p):
        return ((leaf + p) % LEAF, row, col)

    def row_peer(p):
        return (leaf, (row + p) % ROW, col)

    def col_peer(p):
        return (leaf, row, (col + p) % COL)

    def chip_peer(p):
        return (leaf, row, 2 * ((chip + p) % CHIP) + core)

    twin = (leaf, row, col + 1 - 2 * core)
    turned = (leaf, chip, 2 * row + core)

    loads = [
        pltpu.make_async_copy(inv_ref, k.inv_v, k.load.at[0]),
        pltpu.make_async_copy(panel_ref, k.panel_v, k.load.at[1]),
        pltpu.make_async_copy(yc_ref.at[8 * core + chip], k.yc_v, k.load.at[2]),
        pltpu.make_async_copy(cinv_ref.at[:, 0], k.cinv_v.at[0], k.load.at[3]),
        pltpu.make_async_copy(cinv_ref.at[:, 1], k.cinv_v.at[1], k.load.at[4]),
    ]
    for load in loads:
        load.start()

    barrier = pltpu.get_barrier_semaphore()

    def greet(device):
        pl.semaphore_signal(barrier, inc=1, device_id=device, device_id_type=MESH)

    for p in range(1, LEAF):
        greet(leaf_peer(p))
    for p in range(1, ROW):
        greet(row_peer(p))
    for p in range(1, COL):
        greet(col_peer(p))

    @pl.when(chip != row)
    def _():
        greet(turned)

    y = y_ref[...].astype(F32)
    k.ybuf[leaf, row] = jnp.concatenate([y[:, :512], y[:, 512:]], axis=0).astype(BF)

    pl.semaphore_wait(barrier, LEAF - 1 + ROW - 1 + COL - 1 + jnp.where(chip == row, 0, 1))

    exchange = []
    for p in range(1, LEAF):
        slot = k.ybuf.at[leaf, row]
        exchange.append(remote(slot, slot, k.z_s.at[p - 1], k.z_r.at[p - 1], leaf_peer(p)))
        go(exchange[-1])

    def ring_step(h, step):
        copies = []
        for way in range(2):
            at = (row - step + ROW) % ROW if way == 0 else (row + step) % ROW
            leaves = pl.ds(h * LH, LH) if step < 3 else pl.ds(h * LH + way * (LH // 2), LH // 2)
            part = k.ybuf.at[leaves, at]
            copies.append(
                remote(part, part, k.ring_s.at[h, way, step], k.ring_r.at[h, way, step], row_peer(1 if way == 0 else ROW - 1))
            )
        return copies

    for copy in exchange:
        copy.wait_recv()
    ring = {}
    for step in range(4):
        for h in range(NH):
            if step:
                for copy in ring[h]:
                    copy.wait_recv()
            ring[h] = ring_step(h, step)
            for copy in ring[h]:
                go(copy)

    flight = {}

    def send_all(name, h, copies):
        for copy in copies:
            go(copy)
        flight[name, h] = copies

    def arrived(name, h):
        for copy in flight.pop((name, h)):
            copy.wait_recv()

    def root_mm(h):
        if h == 0:
            loads[0].wait()
        for copy in ring.pop(h):
            copy.wait_recv()
        y = k.ybuf[h * LH : (h + 1) * LH].astype(F32)
        total = None
        for half in range(2):
            part = y[:, :, 8 * half : 8 * half + 8, :].reshape(W, 512).astype(BF)
            term = lax.dot_general(
                k.inv_v[:, 512 * half : 512 * half + 512],
                part,
                (((1,), (1,)), ((), ())),
                preferred_element_type=F32,
            )
            total = term if total is None else total + term
        total = total.astype(BF)
        for block in range(2):
            k.xpart[h, :, block] = total[256 * block : 256 * block + 256].reshape(COL, 16, W)
        send_all(
            "x",
            h,
            [
                remote(k.xpart.at[h, (col + p) % COL], k.xin.at[h, p - 1], k.xin_s.at[h, p - 1], k.xin_r.at[h, p - 1], col_peer(p))
                for p in range(1, COL)
            ],
        )

    def root_sum(h):
        arrived("x", h)
        total = k.xpart[h, col].astype(F32)
        for p in range(COL - 1):
            total = total + k.xin[h, p].astype(F32)
        xpair[h][0] = total.astype(BF)
        send_all("swap", h, [remote(xpair[h].at[0], xpair[h].at[1], k.swap_s.at[h], k.swap_r.at[h], leaf_peer(2))])
        root_out(h)

    def root_copy(h, block):
        target = 8 * block + col // 2
        return target, remote(
            xpair[h].at[0, block], k.xo.at[col % 2, h], k.xo_s.at[h, block], k.xo_r.at[h, col % 2], (leaf, row, target)
        )

    def root_out(h):
        for block in range(2):
            target, copy = root_copy(h, block)

            @pl.when(target != col)
            def _():
                copy.start()

            @pl.when(target == col)
            def _():
                k.xo[col % 2, h] = xpair[h][0, block]

    def root_finish(h):
        for block in range(2):
            target, copy = root_copy(h, block)

            @pl.when(target != col)
            def _():
                copy.wait_send()

        for slot in range(2):

            @pl.when(2 * (col % 8) + slot != col)
            def _():
                remote(xpair[h].at[0, 0], k.xo.at[slot, h], k.xo_s.at[h, 0], k.xo_r.at[h, slot], (leaf, row, col)).wait_recv()

            xroot_ref[16 * slot : 16 * slot + 16, h * W : (h + 1) * W] = k.xo[slot, h]

    def y_spread(h):
        arrived("swap", h)
        swapped = jnp.where(map_ref[leaf, 0] // 16 == leaf, 0, 1)
        mine = xg[h].at[pl.ds(2 * row, 2)]
        xg[h][pl.ds(2 * row, 2)] = xpair[h][swapped]
        send_all(
            "g",
            h,
            [remote(mine, mine, k.xg_s.at[h, p - 1], k.xg_r.at[h, p - 1], row_peer(p)) for p in range(1, ROW)],
        )

    def col_spread(h):
        arrived("g", h)
        copies = []
        for p in range(1, COL):
            k.picked[h, p - 1] = xg[h][map_ref[leaf, (col + p) % COL] % 16]
            copies.append(remote(k.picked.at[h, p - 1], k.sel.at[h, col], k.sel_s.at[h, p - 1], k.sel_r.at[h, p - 1], col_peer(p)))
            go(copies[-1])
        flight["sel", h] = copies
        k.sel[h, col] = xg[h][map_ref[leaf, col] % 16]

    def times(tile, right):
        return jnp.dot(tile, right, preferred_element_type=F32).reshape(8, 96, W)

    def panel_mm(h):
        if h == 0:
            loads[1].wait()
        arrived("sel", h)
        right = k.sel[h].reshape(256, W)
        k.pother[h] = times(k.panel_v[1 - core], right).astype(BF)
        send_all("pin", h, [remote(k.pother.at[h], k.pin.at[h], k.pin_s.at[h], k.pin_r.at[h], twin)])
        k.pown[h] = times(k.panel_v[core], right)

    def scatter(h, name, own, inc, out, rx, send, recv):
        copies = []
        for p in range(1, CHIP):
            at = (chip + p) % CHIP
            out[h, p - 1] = (own[h, at] + inc[h, at].astype(F32)).astype(BF)
            copies.append(remote(out.at[h, p - 1], rx.at[h, p - 1], send.at[h, p - 1], recv.at[h, p - 1], chip_peer(p)))
            go(copies[-1])
        flight[name, h] = copies

    def gathered(h, own, inc, rx):
        total = own[h, chip] + inc[h, chip].astype(F32)
        for p in range(CHIP - 1):
            total = total + rx[h, p].astype(F32)
        return total

    def panel_rs(h):
        arrived("pin", h)
        scatter(h, "prx", k.pown, k.pin, k.pout, k.prx, k.prx_s, k.prx_r)

    def turn(h):
        return remote(k.red.at[h], k.rf.at[h, chip], k.turn_s.at[h], k.turn_r.at[h], turned)

    def panel_sum(h):
        if h == 0:
            loads[2].wait()
        arrived("prx", h)
        yc = k.yc_v[:, h * W : (h + 1) * W].astype(F32)
        k.red[h] = (yc - gathered(h, k.pown, k.pin, k.prx)).astype(BF)

        @pl.when(chip != row)
        def _():
            turn(h).start()

        @pl.when(chip == row)
        def _():
            k.rf[h, row] = k.red[h]

    def slab_spread(h):
        @pl.when(chip != row)
        def _():
            turn(h).wait()

        mine = k.rf.at[h, row]
        send_all(
            "rf",
            h,
            [remote(mine, mine, k.rf_s.at[h, p - 1], k.rf_r.at[h, p - 1], row_peer(p)) for p in range(1, ROW)],
        )

    def child_mm(h):
        if h == 0:
            loads[3].wait()
            loads[4].wait()
        arrived("rf", h)
        right = k.rf[h].reshape(768, W)
        k.cother[h] = times(k.cinv_v[1 - core].reshape(768, 768), right).astype(BF)
        send_all("cin", h, [remote(k.cother.at[h], k.cin.at[h], k.cin_s.at[h], k.cin_r.at[h], twin)])
        k.cown[h] = times(k.cinv_v[core].reshape(768, 768), right)

    def child_rs(h):
        arrived("cin", h)
        scatter(h, "crx", k.cown, k.cin, k.cout, k.crx, k.crx_s, k.crx_r)

    def child_sum(h):
        arrived("crx", h)
        xchild_ref[:, h * W : (h + 1) * W] = gathered(h, k.cown, k.cin, k.crx).astype(BF)

    stages = [
        root_mm, root_sum, y_spread, col_spread, panel_mm, panel_rs,
        panel_sum, slab_spread, child_mm, child_rs, child_sum,
    ]
    for t in range(len(stages) + NH - 1):
        for h in range(NH):
            if 0 <= t - h < len(stages):
                stages[t - h](h)
    for h in range(NH):
        root_finish(h)
    for copy in sent:
        copy.wait_send()


def per_device(y_root, root_inverse, block_map, y_child, panel, child_inverse):
    vmem = pl.BlockSpec(memory_space=pltpu.VMEM)
    hbm = pl.BlockSpec(memory_space=pl.ANY)
    x_root, x_child = pl.pallas_call(
        kernel,
        out_shape=(jax.ShapeDtypeStruct((32, 256), BF), jax.ShapeDtypeStruct((96, 256), BF)),
        in_specs=[vmem, hbm, pl.BlockSpec(memory_space=pltpu.SMEM), hbm, hbm, hbm],
        out_specs=(vmem, vmem),
        scratch_shapes=list(SCRATCH.values()),
        compiler_params=pltpu.CompilerParams(collective_id=0, has_side_effects=True, vmem_limit_bytes=56 * 2**20),
    )(
        y_root.T,
        root_inverse,
        block_map,
        y_child.reshape(16, 96, 256),
        panel.reshape(2, 768, 256),
        child_inverse.reshape(8, 2, 96, 768),
    )
    return x_root, x_child[None]


def solution(mesh):
    in_specs = (
        P("col", ("leaf", "row")),
        P(("leaf", "row"), "col"),
        P(),
        P("leaf", "row", None),
        P("leaf", "row", "col"),
        P("leaf", "row", "col"),
    )
    out_specs = (P(("leaf", "row", "col"), None), P("leaf", ("row", "col"), None))
    return jax.shard_map(per_device, mesh=mesh, in_specs=in_specs, out_specs=out_specs, check_vma=False)
```

time: 1340 us -> 95.2 us (0.07)
  waiting for transfers between devices: 1160 us -> 0 us
  Pallas kernels: 0 us -> 91.5 us
  blocking collectives: 78.3 us -> 0 us
  local copies, waits for them, and re-layouts: 74.6 us -> 2.74 us
    all_gather x1 -> x0, waiting for transfers between devices: 815 us -> none  [per_device(): lax.all_gather(x_root, ('leaf', 'row', 'col'), axis=0, tiled=True)]
    psum x2 -> x0, waiting for transfers between devices: 209 us -> none  [the longest x1 134 us: per_device(): lax.psum(jnp.dot(panel_tile, selected, preferred_element_type=jnp.float32...]
    pallas_call x0 -> x1, Pallas kernels: none -> 91.5 us  [per_device(): pl.pallas_call(kernel, out_shape=(jax.ShapeDtypeStruct((32, 256), BF), ja...]
    all_gather x1 -> x0, blocking collectives: 78.3 us -> none  [per_device(): rhs_full = lax.all_gather(y_root, ('leaf', 'row'), axis=1, tiled=True)]
    reduce_scatter x1 -> x0, waiting for transfers between devices: 69.5 us -> none  [per_device(): lax.psum_scatter(jnp.dot(root_inverse, rhs_full, preferred_element_type=j...]
    scatter x1 -> x0, local copies, waits for them, and re-layouts: 69.2 us -> none  [per_device(): selected = zero_rows.at[target].set(shard_rows, mode='drop')]
    unnamed x6 -> x0, waiting for transfers between devices: 67.4 us -> none
  transfers between devices with their start and end apart: 5 -> 0, of which waited for: 5 -> 0; matrix products, arithmetic and copies ran while one was open for 0% -> 0% of each run, Pallas kernels for 0% -> 0%
where the time goes in v1:
time: 95.2 us; the launch traced here: 94.9 us
  Pallas kernels  91.5 us (96%)
  local copies, waits for them, and re-layouts  2.74 us (3%)
    pallas_call x1, Pallas kernels, per_device(): pl.pallas_call(kernel, out_shape=(jax.ShapeDtypeStruct((32, 256), BF), ja...  91.5 us
    unnamed x2, local copies, waits for them, and re-layouts  2.74 us

profile of v1, /device:TPU:1, one launch (start us, length us, event | category | flops | bytes accessed | tf_op | source)
XLA Modules:
  0.0 94.9 jit_solution(444898293430851997)
XLA Ops:
  0.6 91.5 %shard_map.77 = (bf16[32,256]{1,0:T(8,128)(2,1)}, bf16[96,256]{1,0:T(8,128)(2,1)}) custom-call(bf16[8,1024]{1,0:T(8,128)(2,1)} %bitcast.9, bf16[512,1024]{1,0:T(8,128)(2,1)} %inv_ref.1, s32[4,16]{1,0:T(4,128)} %map_ref.1, bf16[16,96,256]{2,1,0:T(8,128)(2,1)} %bitcast.6, bf16[2,768,256]{2,1,0:T(8,128)(2,1)} %bitcast.7, bf16[8,2,96,768]{3,2,1,0:T(8,128)(2,1)} %bitcast.5), custom_call_target="tpu_custom_call" | custom-call | tf_op jit(solution)/shard_map/pallas_call | solution.py:369
  92.1 1.3 %copy.10 = bf16[32,256]{1,0:T(8,128)(2,1)} copy(bf16[32,256]{1,0:T(8,128)(2,1)} %get-tuple-element.8) | data formatting | bytes 32768
  93.5 1.4 %copy.11 = bf16[1,96,256]{2,1,0:T(8,128)(2,1)} copy(bf16[1,96,256]{2,1,0:T(8,128)(2,1)} %bitcast.8) | data formatting | bytes 98304

commit v2 on v1

v2 whole, which is shorter than its diff:
```python
import jax
import jax.numpy as jnp
from jax import lax
from jax.experimental import pallas as pl
from jax.experimental.pallas import tpu as pltpu
from jax.sharding import PartitionSpec as P

MESH = pl.DeviceIdType.MESH
BF, F32 = jnp.bfloat16, jnp.float32

LEAF, ROW, COL, CHIP = 4, 8, 16, 8
NH = 2
W = 256 // NH

DMA = pltpu.SemaphoreType.DMA
SCRATCH = dict(
    inv_v=pltpu.VMEM((512, 1024), BF),
    panel_v=pltpu.VMEM((2, 768, 256), BF),
    cinv_v=pltpu.VMEM((2, 8, 96, 768), BF),
    yc_v=pltpu.VMEM((96, 256), BF),
    load=DMA((5,)),
    ya=pltpu.VMEM((LEAF, ROW, 16, 256), BF),
    yb=pltpu.VMEM((LEAF, ROW, 16, 256), BF),
    ya_s=DMA((LEAF, ROW)),
    ya_r=DMA((LEAF, ROW)),
    yb_s=DMA((LEAF, ROW)),
    yb_r=DMA((LEAF, ROW)),
    xpart=pltpu.VMEM((COL, 2, 16, 256), BF),
    xin=pltpu.VMEM((COL - 1, 2, 16, 256), BF),
    xin_s=DMA((COL - 1,)),
    xin_r=DMA((COL - 1,)),
    xpair=pltpu.VMEM((2, 2, 16, 256), BF),
    swap_s=DMA((1,)),
    swap_r=DMA((1,)),
    xg=pltpu.VMEM((16, 16, 256), BF),
    xg_s=DMA((ROW - 1,)),
    xg_r=DMA((ROW - 1,)),
    picked=pltpu.VMEM((COL - 1, 16, 256), BF),
    sel=pltpu.VMEM((COL, 16, 256), BF),
    sel_s=DMA((COL - 1,)),
    sel_r=DMA((COL - 1,)),
    xo=pltpu.VMEM((2, 16, 256), BF),
    xo_s=DMA((2,)),
    xo_r=DMA((2,)),
    pother=pltpu.VMEM((NH, 8, 96, W), BF),
    pin=pltpu.VMEM((NH, 8, 96, W), BF),
    pin_s=DMA((NH,)),
    pin_r=DMA((NH,)),
    pown=pltpu.VMEM((NH, 8, 96, W), F32),
    pout=pltpu.VMEM((NH, CHIP - 1, 96, W), BF),
    prx=pltpu.VMEM((NH, CHIP - 1, 96, W), BF),
    prx_s=DMA((NH, CHIP - 1)),
    prx_r=DMA((NH, CHIP - 1)),
    red=pltpu.VMEM((NH, 96, W), BF),
    rf=pltpu.VMEM((NH, CHIP, 96, W), BF),
    rf_s=DMA((NH, ROW)),
    rf_r=DMA((NH, CHIP)),
    cother=pltpu.VMEM((NH, 8, 96, W), BF),
    cin=pltpu.VMEM((NH, 8, 96, W), BF),
    cin_s=DMA((NH,)),
    cin_r=DMA((NH,)),
    cown=pltpu.VMEM((NH, 8, 96, W), F32),
    cout=pltpu.VMEM((NH, CHIP - 1, 96, W), BF),
    crx=pltpu.VMEM((NH, CHIP - 1, 96, W), BF),
    crx_s=DMA((NH, CHIP - 1)),
    crx_r=DMA((NH, CHIP - 1)),
)


class Refs:
    pass


def kernel(y_ref, inv_ref, map_ref, yc_ref, panel_ref, cinv_ref, xroot_ref, xchild_ref, *scratch):
    k = Refs()
    for name, ref in zip(SCRATCH, scratch):
        setattr(k, name, ref)
    leaf, row, col = lax.axis_index("leaf"), lax.axis_index("row"), lax.axis_index("col")
    core, chip = col % 2, col // 2
    sent = []

    def remote(src, dst, send, recv, device):
        return pltpu.make_async_remote_copy(
            src_ref=src, dst_ref=dst, send_sem=send, recv_sem=recv, device_id=device, device_id_type=MESH
        )

    def go(copy):
        copy.start()
        sent.append(copy)

    def leaf_peer(p):
        return ((leaf + p) % LEAF, row, col)

    def row_peer(p):
        return (leaf, (row + p) % ROW, col)

    def col_peer(p):
        return (leaf, row, (col + p) % COL)

    def chip_peer(p):
        return (leaf, row, 2 * ((chip + p) % CHIP) + core)

    twin = (leaf, row, col + 1 - 2 * core)

    def band_peer(p):
        return (leaf, (row + p) % ROW, 2 * row + core)


    loads = [
        pltpu.make_async_copy(inv_ref, k.inv_v, k.load.at[0]),
        pltpu.make_async_copy(panel_ref, k.panel_v, k.load.at[1]),
        pltpu.make_async_copy(yc_ref.at[8 * core + chip], k.yc_v, k.load.at[2]),
        pltpu.make_async_copy(cinv_ref.at[:, 0], k.cinv_v.at[0], k.load.at[3]),
        pltpu.make_async_copy(cinv_ref.at[:, 1], k.cinv_v.at[1], k.load.at[4]),
    ]
    for load in loads:
        load.start()

    barrier = pltpu.get_barrier_semaphore()

    def greet(device):
        pl.semaphore_signal(barrier, inc=1, device_id=device, device_id_type=MESH)

    for p in range(1, LEAF):
        greet(leaf_peer(p))
    for p in range(1, ROW):
        greet(row_peer(p))
    for p in range(1, COL):
        greet(col_peer(p))

    @pl.when(chip != row)
    def _():
        for p in range(1, CHIP):
            greet((leaf, chip, 2 * ((chip + p) % CHIP) + core))

    y = y_ref[...].astype(F32)
    for part, at in ((k.ya, 0), (k.yb, 512)):
        part[leaf, row] = jnp.concatenate([y[:, at : at + 256], y[:, at + 256 : at + 512]], axis=0).astype(BF)

    pl.semaphore_wait(barrier, LEAF - 1 + ROW - 1 + COL - 1 + jnp.where(chip == row, 0, CHIP - 1))

    def a_copy(a, p):
        if p == 0:
            part = k.ya.at[leaf, row]
            return remote(part, part, k.ya_s.at[a, 0], k.ya_r.at[a, 0], leaf_peer(a))
        part = k.ya.at[(leaf - a + LEAF) % LEAF, row]
        return remote(part, part, k.ya_s.at[a, p], k.ya_r.at[a, p], row_peer(p))

    def b_copy(a, p):
        if a == 0:
            part = k.yb.at[leaf, row]
            return remote(part, part, k.yb_s.at[0, p], k.yb_r.at[0, p], row_peer(p))
        part = k.yb.at[leaf, (row - p + ROW) % ROW]
        return remote(part, part, k.yb_s.at[a, p], k.yb_r.at[a, p], leaf_peer(a))

    leaf_order, row_order = (1, 3, 2), (1, 7, 2, 6, 3, 5, 4)
    for a in leaf_order:
        go(a_copy(a, 0))
    for p in row_order:
        go(b_copy(0, p))
    for a in leaf_order:
        go(b_copy(a, 0))
    for p in row_order:
        go(a_copy(0, p))
    near = [("b", 1), ("b", 7), ("a", 1), ("a", 3), ("b", 2), ("b", 6), ("b", 3), ("b", 5), ("a", 2), ("b", 4)]
    for which, n in near:
        if which == "a":
            a_copy(n, 0).wait_recv()
            for p in row_order:
                go(a_copy(n, p))
        else:
            b_copy(0, n).wait_recv()
            for a in leaf_order:
                go(b_copy(a, n))

    flight = {}

    def send_all(name, h, copies):
        for copy in copies:
            go(copy)
        flight[name, h] = copies

    def arrived(name, h):
        for copy in flight.pop((name, h)):
            copy.wait_recv()

    def root_mm():
        loads[0].wait()
        total = None
        for half, part in enumerate((k.ya, k.yb)):
            for a in range(LEAF):
                for p in range(ROW):
                    if half == 0 and p:
                        a_copy(a, p).wait_recv()
                    if half == 1 and a:
                        b_copy(a, p).wait_recv()
            y = part[...].astype(F32)
            for sub in range(2):
                at = 512 * half + 256 * sub
                term = lax.dot_general(
                    k.inv_v[:, at : at + 256],
                    y[:, :, 8 * sub : 8 * sub + 8, :].reshape(256, 256).astype(BF),
                    (((1,), (1,)), ((), ())),
                    preferred_element_type=F32,
                )
                total = term if total is None else total + term
        total = total.astype(BF)
        for block in range(2):
            k.xpart[:, block] = total[256 * block : 256 * block + 256].reshape(COL, 16, 256)
        send_all(
            "x",
            0,
            [
                remote(k.xpart.at[(col + p) % COL], k.xin.at[p - 1], k.xin_s.at[p - 1], k.xin_r.at[p - 1], col_peer(p))
                for p in range(1, COL)
            ],
        )

    def root_sum():
        arrived("x", 0)
        total = k.xpart[col].astype(F32)
        for p in range(COL - 1):
            total = total + k.xin[p].astype(F32)
        k.xpair[0] = total.astype(BF)
        send_all("swap", 0, [remote(k.xpair.at[0], k.xpair.at[1], k.swap_s.at[0], k.swap_r.at[0], leaf_peer(2))])
        root_out()

    def root_copy(block):
        target = 8 * block + col // 2
        return target, remote(
            k.xpair.at[0, block], k.xo.at[col % 2], k.xo_s.at[block], k.xo_r.at[col % 2], (leaf, row, target)
        )

    def root_out():
        for block in range(2):
            target, copy = root_copy(block)

            @pl.when(target != col)
            def _():
                copy.start()

            @pl.when(target == col)
            def _():
                k.xo[col % 2] = k.xpair[0, block]

    def root_finish():
        for block in range(2):
            target, copy = root_copy(block)

            @pl.when(target != col)
            def _():
                copy.wait_send()

        for slot in range(2):

            @pl.when(2 * (col % 8) + slot != col)
            def _():
                remote(k.xpair.at[0, 0], k.xo.at[slot], k.xo_s.at[0], k.xo_r.at[slot], (leaf, row, col)).wait_recv()

            xroot_ref[16 * slot : 16 * slot + 16, :] = k.xo[slot]

    def y_spread():
        arrived("swap", 0)
        swapped = jnp.where(map_ref[leaf, 0] // 16 == leaf, 0, 1)
        mine = k.xg.at[pl.ds(2 * row, 2)]
        k.xg[pl.ds(2 * row, 2)] = k.xpair[swapped]
        send_all(
            "g",
            0,
            [remote(mine, mine, k.xg_s.at[p - 1], k.xg_r.at[p - 1], row_peer(p)) for p in range(1, ROW)],
        )

    def col_spread():
        arrived("g", 0)
        copies = []
        for p in range(1, COL):
            k.picked[p - 1] = k.xg[map_ref[leaf, (col + p) % COL] % 16]
            copies.append(remote(k.picked.at[p - 1], k.sel.at[col], k.sel_s.at[p - 1], k.sel_r.at[p - 1], col_peer(p)))
            go(copies[-1])
        flight["sel", 0] = copies
        k.sel[col] = k.xg[map_ref[leaf, col] % 16]

    def times(tile, right):
        return jnp.dot(tile, right, preferred_element_type=F32).reshape(8, 96, W)

    def panel_mm(h):
        if h == 0:
            loads[1].wait()
            arrived("sel", 0)
        right = k.sel[:, :, h * W : (h + 1) * W].reshape(256, W)
        k.pother[h] = times(k.panel_v[1 - core], right).astype(BF)
        send_all("pin", h, [remote(k.pother.at[h], k.pin.at[h], k.pin_s.at[h], k.pin_r.at[h], twin)])
        k.pown[h] = times(k.panel_v[core], right)

    def scatter(h, name, own, inc, out, rx, send, recv):
        copies = []
        for p in range(1, CHIP):
            at = (chip + p) % CHIP
            out[h, p - 1] = (own[h, at] + inc[h, at].astype(F32)).astype(BF)
            copies.append(remote(out.at[h, p - 1], rx.at[h, p - 1], send.at[h, p - 1], recv.at[h, p - 1], chip_peer(p)))
            go(copies[-1])
        flight[name, h] = copies

    def gathered(h, own, inc, rx):
        total = own[h, chip] + inc[h, chip].astype(F32)
        for p in range(CHIP - 1):
            total = total + rx[h, p].astype(F32)
        return total

    def panel_rs(h):
        arrived("pin", h)
        scatter(h, "prx", k.pown, k.pin, k.pout, k.prx, k.prx_s, k.prx_r)

    def band_copy(h, p):
        return remote(k.red.at[h], k.rf.at[h, chip], k.rf_s.at[h, p], k.rf_r.at[h, chip], band_peer(p))

    def panel_sum(h):
        if h == 0:
            loads[2].wait()
        arrived("prx", h)
        yc = k.yc_v[:, h * W : (h + 1) * W].astype(F32)
        k.red[h] = (yc - gathered(h, k.pown, k.pin, k.prx)).astype(BF)
        for p in (4, 3, 5, 2, 6, 1, 7):
            go(band_copy(h, p))

        @pl.when(chip != row)
        def _():
            band_copy(h, 0).start()

        @pl.when(chip == row)
        def _():
            k.rf[h, chip] = k.red[h]

    def band_arrived(h):
        def wait(q):
            remote(k.red.at[h], k.rf.at[h, q], k.rf_s.at[h, 0], k.rf_r.at[h, q], band_peer(0)).wait_recv()

        for p in range(1, CHIP):
            wait((chip + p) % CHIP)

        @pl.when(chip != row)
        def _():
            wait(chip)
            band_copy(h, 0).wait_send()

    def child_mm(h):
        if h == 0:
            loads[3].wait()
            loads[4].wait()
        band_arrived(h)
        right = k.rf[h].reshape(768, W)
        k.cother[h] = times(k.cinv_v[1 - core].reshape(768, 768), right).astype(BF)
        send_all("cin", h, [remote(k.cother.at[h], k.cin.at[h], k.cin_s.at[h], k.cin_r.at[h], twin)])
        k.cown[h] = times(k.cinv_v[core].reshape(768, 768), right)

    def child_rs(h):
        arrived("cin", h)
        scatter(h, "crx", k.cown, k.cin, k.cout, k.crx, k.crx_s, k.crx_r)

    def child_sum(h):
        arrived("crx", h)
        xchild_ref[:, h * W : (h + 1) * W] = gathered(h, k.cown, k.cin, k.crx).astype(BF)

    root_mm()
    root_sum()
    y_spread()
    col_spread()
    stages = [panel_mm, panel_rs, panel_sum, child_mm, child_rs, child_sum]
    for t in range(len(stages) + NH - 1):
        for h in range(NH):
            if 0 <= t - h < len(stages):
                stages[t - h](h)
    root_finish()
    for copy in sent:
        copy.wait_send()


def per_device(y_root, root_inverse, block_map, y_child, panel, child_inverse):
    vmem = pl.BlockSpec(memory_space=pltpu.VMEM)
    hbm = pl.BlockSpec(memory_space=pl.ANY)
    x_root, x_child = pl.pallas_call(
        kernel,
        out_shape=(jax.ShapeDtypeStruct((32, 256), BF), jax.ShapeDtypeStruct((96, 256), BF)),
        in_specs=[vmem, hbm, pl.BlockSpec(memory_space=pltpu.SMEM), hbm, hbm, hbm],
        out_specs=(vmem, vmem),
        scratch_shapes=list(SCRATCH.values()),
        compiler_params=pltpu.CompilerParams(collective_id=0, has_side_effects=True, vmem_limit_bytes=56 * 2**20),
    )(
        y_root.T,
        root_inverse,
        block_map,
        y_child.reshape(16, 96, 256),
        panel.reshape(2, 768, 256),
        child_inverse.reshape(8, 2, 96, 768),
    )
    return x_root, x_child[None]


def solution(mesh):
    in_specs = (
        P("col", ("leaf", "row")),
        P(("leaf", "row"), "col"),
        P(),
        P("leaf", "row", None),
        P("leaf", "row", "col"),
        P("leaf", "row", "col"),
    )
    out_specs = (P(("leaf", "row", "col"), None), P("leaf", ("row", "col"), None))
    return jax.shard_map(per_device, mesh=mesh, in_specs=in_specs, out_specs=out_specs, check_vma=False)
```

time: 95.2 us -> 84.5 us (0.89)
  Pallas kernels: 91.5 us -> 80.8 us
    pallas_call x1, Pallas kernels: 91.5 us -> 80.8 us  [per_device(): pl.pallas_call(kernel, out_shape=(jax.ShapeDtypeStruct((32, 256), BF), ja...]
where the time goes in v2:
time: 84.5 us; the launch traced here: 84.2 us
  Pallas kernels  80.8 us (96%)
  local copies, waits for them, and re-layouts  2.74 us (3%)
    pallas_call x1, Pallas kernels, per_device(): pl.pallas_call(kernel, out_shape=(jax.ShapeDtypeStruct((32, 256), BF), ja...  80.8 us
    unnamed x2, local copies, waits for them, and re-layouts  2.74 us

profile of v2, /device:TPU:1, one launch (start us, length us, event | category | flops | bytes accessed | tf_op | source)
XLA Modules:
  0.0 84.2 jit_solution(7270309478495321351)
XLA Ops:
  0.6 80.8 %shard_map.77 = (bf16[32,256]{1,0:T(8,128)(2,1)}, bf16[96,256]{1,0:T(8,128)(2,1)}) custom-call(bf16[8,1024]{1,0:T(8,128)(2,1)} %bitcast.9, bf16[512,1024]{1,0:T(8,128)(2,1)} %inv_ref.1, s32[4,16]{1,0:T(4,128)} %map_ref.1, bf16[16,96,256]{2,1,0:T(8,128)(2,1)} %bitcast.6, bf16[2,768,256]{2,1,0:T(8,128)(2,1)} %bitcast.7, bf16[8,2,96,768]{3,2,1,0:T(8,128)(2,1)} %bitcast.5), custom_call_target="tpu_custom_call" | custom-call | tf_op jit(solution)/shard_map/pallas_call | solution.py:381
  81.4 1.3 %copy.10 = bf16[32,256]{1,0:T(8,128)(2,1)} copy(bf16[32,256]{1,0:T(8,128)(2,1)} %get-tuple-element.8) | data formatting | bytes 32768
  82.7 1.4 %copy.11 = bf16[1,96,256]{2,1,0:T(8,128)(2,1)} copy(bf16[1,96,256]{2,1,0:T(8,128)(2,1)} %bitcast.8) | data formatting | bytes 98304

commit v3 on v2

--- a/solution.py
+++ b/solution.py
@@ -18,7 +18,9 @@
     panel_v=pltpu.VMEM((2, 768, 256), BF),
     cinv_v=pltpu.VMEM((2, 8, 96, 768), BF),
     yc_v=pltpu.VMEM((96, 256), BF),
-    load=DMA((5,)),
+    y_v=pltpu.VMEM((8, 1024), BF),
+    map_v=pltpu.SMEM((4, 16), jnp.int32),
+    load=DMA((7,)),
     ya=pltpu.VMEM((LEAF, ROW, 16, 256), BF),
     yb=pltpu.VMEM((LEAF, ROW, 16, 256), BF),
     ya_s=DMA((LEAF, ROW)),
@@ -71,7 +73,7 @@
     pass
 
 
-def kernel(y_ref, inv_ref, map_ref, yc_ref, panel_ref, cinv_ref, xroot_ref, xchild_ref, *scratch):
+def kernel(y_ref, inv_ref, map_ref, yc_ref, panel_ref, cinv_ref, both_ref, *scratch):
     k = Refs()
     for name, ref in zip(SCRATCH, scratch):
         setattr(k, name, ref)
@@ -87,6 +89,10 @@
     def go(copy):
         copy.start()
         sent.append(copy)
+
+    def drain(keep):
+        while len(sent) > keep:
+            sent.pop(0).wait_send()
 
     def leaf_peer(p):
         return ((leaf + p) % LEAF, row, col)
@@ -113,7 +119,11 @@
         pltpu.make_async_copy(cinv_ref.at[:, 0], k.cinv_v.at[0], k.load.at[3]),
         pltpu.make_async_copy(cinv_ref.at[:, 1], k.cinv_v.at[1], k.load.at[4]),
     ]
-    for load in loads:
+    small = [
+        pltpu.make_async_copy(y_ref, k.y_v, k.load.at[5]),
+        pltpu.make_async_copy(map_ref, k.map_v, k.load.at[6]),
+    ]
+    for load in small + loads:
         load.start()
 
     barrier = pltpu.get_barrier_semaphore()
@@ -133,7 +143,8 @@
         for p in range(1, CHIP):
             greet((leaf, chip, 2 * ((chip + p) % CHIP) + core))
 
-    y = y_ref[...].astype(F32)
+    small[0].wait()
+    y = k.y_v[...].astype(F32)
     for part, at in ((k.ya, 0), (k.yb, 512)):
         part[leaf, row] = jnp.concatenate([y[:, at : at + 256], y[:, at + 256 : at + 512]], axis=0).astype(BF)
 
@@ -179,6 +190,8 @@
         for copy in copies:
             go(copy)
         flight[name, h] = copies
+        if name in ("swap", "g"):
+            drain(len(copies) + COL)
 
     def arrived(name, h):
         for copy in flight.pop((name, h)):
@@ -257,11 +270,12 @@
             def _():
                 remote(k.xpair.at[0, 0], k.xo.at[slot], k.xo_s.at[0], k.xo_r.at[slot], (leaf, row, col)).wait_recv()
 
-            xroot_ref[16 * slot : 16 * slot + 16, :] = k.xo[slot]
+            both_ref[16 * slot : 16 * slot + 16, :] = k.xo[slot]
 
     def y_spread():
         arrived("swap", 0)
-        swapped = jnp.where(map_ref[leaf, 0] // 16 == leaf, 0, 1)
+        small[1].wait()
+        swapped = jnp.where(k.map_v[leaf, 0] // 16 == leaf, 0, 1)
         mine = k.xg.at[pl.ds(2 * row, 2)]
         k.xg[pl.ds(2 * row, 2)] = k.xpair[swapped]
         send_all(
@@ -272,13 +286,16 @@
 
     def col_spread():
         arrived("g", 0)
-        copies = []
         for p in range(1, COL):
-            k.picked[p - 1] = k.xg[map_ref[leaf, (col + p) % COL] % 16]
-            copies.append(remote(k.picked.at[p - 1], k.sel.at[col], k.sel_s.at[p - 1], k.sel_r.at[p - 1], col_peer(p)))
-            go(copies[-1])
+            k.picked[p - 1] = k.xg[k.map_v[leaf, (col + p) % COL] % 16]
+        copies = [
+            remote(k.picked.at[p - 1], k.sel.at[col], k.sel_s.at[p - 1], k.sel_r.at[p - 1], col_peer(p)) for p in range(1, COL)
+        ]
+        for copy in copies:
+            go(copy)
         flight["sel", 0] = copies
-        k.sel[col] = k.xg[map_ref[leaf, col] % 16]
+        k.sel[col] = k.xg[k.map_v[leaf, col] % 16]
+        drain(COL - 1)
 
     def times(tile, right):
         return jnp.dot(tile, right, preferred_element_type=F32).reshape(8, 96, W)
@@ -294,12 +311,13 @@
 
     def scatter(h, name, own, inc, out, rx, send, recv):
         copies = []
-        for p in range(1, CHIP):
+        for p in (2, 6, 1, 3, 5, 7, 4):
             at = (chip + p) % CHIP
             out[h, p - 1] = (own[h, at] + inc[h, at].astype(F32)).astype(BF)
             copies.append(remote(out.at[h, p - 1], rx.at[h, p - 1], send.at[h, p - 1], recv.at[h, p - 1], chip_peer(p)))
             go(copies[-1])
         flight[name, h] = copies
+        drain(2 * CHIP)
 
     def gathered(h, own, inc, rx):
         total = own[h, chip] + inc[h, chip].astype(F32)
@@ -330,6 +348,8 @@
         @pl.when(chip == row)
         def _():
             k.rf[h, chip] = k.red[h]
+
+        drain(2 * CHIP)
 
     def band_arrived(h):
         def wait(q):
@@ -359,17 +379,16 @@
 
     def child_sum(h):
         arrived("crx", h)
-        xchild_ref[:, h * W : (h + 1) * W] = gathered(h, k.cown, k.cin, k.crx).astype(BF)
+        both_ref[32:, h * W : (h + 1) * W] = gathered(h, k.cown, k.cin, k.crx).astype(BF)
 
     root_mm()
     root_sum()
     y_spread()
     col_spread()
     stages = [panel_mm, panel_rs, panel_sum, child_mm, child_rs, child_sum]
-    for t in range(len(stages) + NH - 1):
+    for stage in stages:
         for h in range(NH):
-            if 0 <= t - h < len(stages):
-                stages[t - h](h)
+            stage(h)
     root_finish()
     for copy in sent:
         copy.wait_send()
@@ -378,11 +397,11 @@
 def per_device(y_root, root_inverse, block_map, y_child, panel, child_inverse):
     vmem = pl.BlockSpec(memory_space=pltpu.VMEM)
     hbm = pl.BlockSpec(memory_space=pl.ANY)
-    x_root, x_child = pl.pallas_call(
+    both = pl.pallas_call(
         kernel,
-        out_shape=(jax.ShapeDtypeStruct((32, 256), BF), jax.ShapeDtypeStruct((96, 256), BF)),
-        in_specs=[vmem, hbm, pl.BlockSpec(memory_space=pltpu.SMEM), hbm, hbm, hbm],
-        out_specs=(vmem, vmem),
+        out_shape=jax.ShapeDtypeStruct((128, 256), BF),
+        in_specs=[hbm] * 6,
+        out_specs=vmem,
         scratch_shapes=list(SCRATCH.values()),
         compiler_params=pltpu.CompilerParams(collective_id=0, has_side_effects=True, vmem_limit_bytes=56 * 2**20),
     )(
@@ -393,7 +412,7 @@
         panel.reshape(2, 768, 256),
         child_inverse.reshape(8, 2, 96, 768),
     )
-    return x_root, x_child[None]
+    return both[:32], both[32:][None]
 
 
 def solution(mesh):

time: 84.5 us -> 78.7 us (0.931)
  Pallas kernels: 80.8 us -> 75 us
    pallas_call x1, Pallas kernels: 80.8 us -> 75 us  [per_device(): pl.pallas_call(kernel, out_shape=jax.ShapeDtypeStruct((128, 256), BF), in...]
    unnamed x2 -> x0, local copies, waits for them, and re-layouts: 2.74 us -> none
    broadcast_in_dim x0 -> x1, local copies, waits for them, and re-layouts: none -> 1.42 us  [per_device(): return (both[:32], both[32:][None])]
    slice x0 -> x1, local copies, waits for them, and re-layouts: none -> 1.32 us  [per_device(): return (both[:32], both[32:][None])]
where the time goes in v3:
time: 78.7 us; the launch traced here: 78.4 us
  Pallas kernels  75 us (95%)
  local copies, waits for them, and re-layouts  2.74 us (3%)
    pallas_call x1, Pallas kernels, per_device(): pl.pallas_call(kernel, out_shape=jax.ShapeDtypeStruct((128, 256), BF), in...  75 us

profile of v3, /device:TPU:1, one launch (start us, length us, event | category | flops | bytes accessed | tf_op | source)
XLA Modules:
  0.0 78.4 jit_solution(9019904615281271710)
XLA Ops:
  0.6 75.0 %shard_map.77 = bf16[128,256]{1,0:T(8,128)(2,1)} custom-call(bf16[8,1024]{1,0:T(8,128)(2,1)} %bitcast.9, bf16[512,1024]{1,0:T(8,128)(2,1)} %inv_ref.1, s32[4,16]{1,0:T(4,128)} %map_ref.1, bf16[16,96,256]{2,1,0:T(8,128)(2,1)} %bitcast.7, bf16[2,768,256]{2,1,0:T(8,128)(2,1)} %bitcast.8, bf16[8,2,96,768]{3,2,1,0:T(8,128)(2,1)} %bitcast.6), custom_call_target="tpu_custom_call" | custom-call | tf_op jit(solution)/shard_map/pallas_call | solution.py:400
  75.6 1.3 %slice.6 = bf16[32,256]{1,0:T(8,128)(2,1)} slice(bf16[128,256]{1,0:T(8,128)(2,1)} %shard_map.77), slice={[0:32], [0:256]} | slice | bytes 32768 | tf_op jit(solution)/shard_map/slice | solution.py:415
  77.0 1.4 %slice_bitcast_fusion = bf16[1,96,256]{2,1,0:T(8,128)(2,1)} fusion(bf16[128,256]{1,0:T(8,128)(2,1)} %shard_map.77), kind=kLoop, calls=%fused_computation | loop fusion | bytes 98304 | tf_op jit(solution)/shard_map/broadcast_in_dim | solution.py:415

commit v4 on v3

--- a/solution.py
+++ b/solution.py
@@ -27,23 +27,23 @@
     ya_r=DMA((LEAF, ROW)),
     yb_s=DMA((LEAF, ROW)),
     yb_r=DMA((LEAF, ROW)),
-    xpart=pltpu.VMEM((COL, 2, 16, 256), BF),
-    xin=pltpu.VMEM((COL - 1, 2, 16, 256), BF),
-    xin_s=DMA((COL - 1,)),
-    xin_r=DMA((COL - 1,)),
-    xpair=pltpu.VMEM((2, 2, 16, 256), BF),
-    swap_s=DMA((1,)),
-    swap_r=DMA((1,)),
-    xg=pltpu.VMEM((16, 16, 256), BF),
-    xg_s=DMA((ROW - 1,)),
-    xg_r=DMA((ROW - 1,)),
-    picked=pltpu.VMEM((COL - 1, 16, 256), BF),
-    sel=pltpu.VMEM((COL, 16, 256), BF),
-    sel_s=DMA((COL - 1,)),
-    sel_r=DMA((COL - 1,)),
-    xo=pltpu.VMEM((2, 16, 256), BF),
-    xo_s=DMA((2,)),
-    xo_r=DMA((2,)),
+    xpart=pltpu.VMEM((NH, COL, 2, 16, W), BF),
+    xin=pltpu.VMEM((NH, COL - 1, 2, 16, W), BF),
+    xin_s=DMA((NH, COL - 1)),
+    xin_r=DMA((NH, COL - 1)),
+    **{f"xpair{h}": pltpu.VMEM((2, 2, 16, W), BF) for h in range(NH)},
+    swap_s=DMA((NH,)),
+    swap_r=DMA((NH,)),
+    **{f"xg{h}": pltpu.VMEM((16, 16, W), BF) for h in range(NH)},
+    xg_s=DMA((NH, ROW - 1)),
+    xg_r=DMA((NH, ROW - 1)),
+    picked=pltpu.VMEM((NH, COL - 1, 16, W), BF),
+    sel=pltpu.VMEM((NH, COL, 16, W), BF),
+    sel_s=DMA((NH, COL - 1)),
+    sel_r=DMA((NH, COL - 1)),
+    xo=pltpu.VMEM((2, NH, 16, W), BF),
+    xo_s=DMA((NH, 2)),
+    xo_r=DMA((NH, 2)),
     pother=pltpu.VMEM((NH, 8, 96, W), BF),
     pin=pltpu.VMEM((NH, 8, 96, W), BF),
     pin_s=DMA((NH,)),
@@ -77,6 +77,8 @@
     k = Refs()
     for name, ref in zip(SCRATCH, scratch):
         setattr(k, name, ref)
+    xpair = [getattr(k, f"xpair{h}") for h in range(NH)]
+    xg = [getattr(k, f"xg{h}") for h in range(NH)]
     leaf, row, col = lax.axis_index("leaf"), lax.axis_index("row"), lax.axis_index("col")
     core, chip = col % 2, col // 2
     sent = []
@@ -218,35 +220,38 @@
                 )
                 total = term if total is None else total + term
         total = total.astype(BF)
-        for block in range(2):
-            k.xpart[:, block] = total[256 * block : 256 * block + 256].reshape(COL, 16, 256)
-        send_all(
-            "x",
-            0,
-            [
-                remote(k.xpart.at[(col + p) % COL], k.xin.at[p - 1], k.xin_s.at[p - 1], k.xin_r.at[p - 1], col_peer(p))
-                for p in range(1, COL)
-            ],
-        )
-
-    def root_sum():
-        arrived("x", 0)
-        total = k.xpart[col].astype(F32)
+        for h in range(NH):
+            for block in range(2):
+                k.xpart[h, :, block] = total[256 * block : 256 * block + 256, h * W : (h + 1) * W].reshape(COL, 16, W)
+            send_all(
+                "x",
+                h,
+                [
+                    remote(
+                        k.xpart.at[h, (col + p) % COL], k.xin.at[h, p - 1], k.xin_s.at[h, p - 1], k.xin_r.at[h, p - 1], col_peer(p)
+                    )
+                    for p in range(1, COL)
+                ],
+            )
+
+    def root_sum(h):
+        arrived("x", h)
+        total = k.xpart[h, col].astype(F32)
         for p in range(COL - 1):
-            total = total + k.xin[p].astype(F32)
-        k.xpair[0] = total.astype(BF)
-        send_all("swap", 0, [remote(k.xpair.at[0], k.xpair.at[1], k.swap_s.at[0], k.swap_r.at[0], leaf_peer(2))])
-        root_out()
-
-    def root_copy(block):
+            total = total + k.xin[h, p].astype(F32)
+        xpair[h][0] = total.astype(BF)
+        send_all("swap", h, [remote(xpair[h].at[0], xpair[h].at[1], k.swap_s.at[h], k.swap_r.at[h], leaf_peer(2))])
+        root_out(h)
+
+    def root_copy(h, block):
         target = 8 * block + col // 2
         return target, remote(
-            k.xpair.at[0, block], k.xo.at[col % 2], k.xo_s.at[block], k.xo_r.at[col % 2], (leaf, row, target)
+            xpair[h].at[0, block], k.xo.at[col % 2, h], k.xo_s.at[h, block], k.xo_r.at[h, col % 2], (leaf, row, target)
         )
 
-    def root_out():
+    def root_out(h):
         for block in range(2):
-            target, copy = root_copy(block)
+            target, copy = root_copy(h, block)
 
             @pl.when(target != col)
             def _():
@@ -254,11 +259,11 @@
 
             @pl.when(target == col)
             def _():
-                k.xo[col % 2] = k.xpair[0, block]
-
-    def root_finish():
+                k.xo[col % 2, h] = xpair[h][0, block]
+
+    def root_finish(h):
         for block in range(2):
-            target, copy = root_copy(block)
+            target, copy = root_copy(h, block)
 
             @pl.when(target != col)
             def _():
@@ -268,34 +273,33 @@
 
             @pl.when(2 * (col % 8) + slot != col)
             def _():
-                remote(k.xpair.at[0, 0], k.xo.at[slot], k.xo_s.at[0], k.xo_r.at[slot], (leaf, row, col)).wait_recv()
-
-            both_ref[16 * slot : 16 * slot + 16, :] = k.xo[slot]
-
-    def y_spread():
-        arrived("swap", 0)
-        small[1].wait()
+                remote(xpair[h].at[0, 0], k.xo.at[slot, h], k.xo_s.at[h, 0], k.xo_r.at[h, slot], (leaf, row, col)).wait_recv()
+
+            both_ref[16 * slot : 16 * slot + 16, h * W : (h + 1) * W] = k.xo[slot, h]
+
+    def y_spread(h):
+        arrived("swap", h)
+        if h == 0:
+            small[1].wait()
         swapped = jnp.where(k.map_v[leaf, 0] // 16 == leaf, 0, 1)
-        mine = k.xg.at[pl.ds(2 * row, 2)]
-        k.xg[pl.ds(2 * row, 2)] = k.xpair[swapped]
+        mine = xg[h].at[pl.ds(2 * row, 2)]
+        xg[h][pl.ds(2 * row, 2)] = xpair[h][swapped]
         send_all(
             "g",
-            0,
-            [remote(mine, mine, k.xg_s.at[p - 1], k.xg_r.at[p - 1], row_peer(p)) for p in range(1, ROW)],
+            h,
+            [remote(mine, mine, k.xg_s.at[h, p - 1], k.xg_r.at[h, p - 1], row_peer(p)) for p in (4, 3, 5, 2, 6, 1, 7)],
         )
 
-    def col_spread():
-        arrived("g", 0)
+    def col_spread(h):
+        arrived("g", h)
         for p in range(1, COL):
-            k.picked[p - 1] = k.xg[k.map_v[leaf, (col + p) % COL] % 16]
+            k.picked[h, p - 1] = xg[h][k.map_v[leaf, (col + p) % COL] % 16]
         copies = [
-            remote(k.picked.at[p - 1], k.sel.at[col], k.sel_s.at[p - 1], k.sel_r.at[p - 1], col_peer(p)) for p in range(1, COL)
+            remote(k.picked.at[h, p - 1], k.sel.at[h, col], k.sel_s.at[h, p - 1], k.sel_r.at[h, p - 1], col_peer(p))
+            for p in range(1, COL)
         ]
-        for copy in copies:
-            go(copy)
-        flight["sel", 0] = copies
-        k.sel[col] = k.xg[k.map_v[leaf, col] % 16]
-        drain(COL - 1)
+        send_all("sel", h, copies)
+        k.sel[h, col] = xg[h][k.map_v[leaf, col] % 16]
 
     def times(tile, right):
         return jnp.dot(tile, right, preferred_element_type=F32).reshape(8, 96, W)
@@ -303,8 +307,8 @@
     def panel_mm(h):
         if h == 0:
             loads[1].wait()
-            arrived("sel", 0)
-        right = k.sel[:, :, h * W : (h + 1) * W].reshape(256, W)
+        arrived("sel", h)
+        right = k.sel[h].reshape(256, W)
         k.pother[h] = times(k.panel_v[1 - core], right).astype(BF)
         send_all("pin", h, [remote(k.pother.at[h], k.pin.at[h], k.pin_s.at[h], k.pin_r.at[h], twin)])
         k.pown[h] = times(k.panel_v[core], right)
@@ -382,14 +386,12 @@
         both_ref[32:, h * W : (h + 1) * W] = gathered(h, k.cown, k.cin, k.crx).astype(BF)
 
     root_mm()
-    root_sum()
-    y_spread()
-    col_spread()
-    stages = [panel_mm, panel_rs, panel_sum, child_mm, child_rs, child_sum]
+    stages = [root_sum, y_spread, col_spread, panel_mm, panel_rs, panel_sum, child_mm, child_rs, child_sum]
     for stage in stages:
         for h in range(NH):
             stage(h)
-    root_finish()
+            if stage is panel_sum:
+                root_finish(h)
     for copy in sent:
         copy.wait_send()
 
@@ -412,7 +414,16 @@
         panel.reshape(2, 768, 256),
         child_inverse.reshape(8, 2, 96, 768),
     )
-    return both[:32], both[32:][None]
+    def split(both_ref, root_ref, child_ref):
+        root_ref[...] = both_ref[:32]
+        child_ref[0] = both_ref[32:]
+
+    return pl.pallas_call(
+        split,
+        out_shape=(jax.ShapeDtypeStruct((32, 256), BF), jax.ShapeDtypeStruct((1, 96, 256), BF)),
+        in_specs=[vmem],
+        out_specs=(vmem, vmem),
+    )(both)
 
 
 def solution(mesh):

time: 78.7 us -> 76.6 us (0.973)
  local copies, waits for them, and re-layouts: 2.74 us -> 0 us
  Pallas kernels: 75 us -> 75.8 us
    pallas_call x0 -> x1, Pallas kernels: none -> 1.47 us  [per_device(): pl.pallas_call(split, out_shape=(jax.ShapeDtypeStruct((32, 256), BF), jax...]
    broadcast_in_dim x1 -> x0, local copies, waits for them, and re-layouts: 1.42 us -> none  [per_device(): return (both[:32], both[32:][None])]
    slice x1 -> x0, local copies, waits for them, and re-layouts: 1.32 us -> none  [per_device(): return (both[:32], both[32:][None])]
where the time goes in v4:
time: 76.6 us; the launch traced here: 76.4 us
  Pallas kernels  75.8 us (99%)
    pallas_call x1, Pallas kernels, per_device(): pl.pallas_call(kernel, out_shape=jax.ShapeDtypeStruct((128, 256), BF), in...  74.3 us

profile of v4, /device:TPU:1, one launch (start us, length us, event | category | flops | bytes accessed | tf_op | source)
XLA Modules:
  0.0 76.4 jit_solution(11396844706620124888)
XLA Ops:
  0.6 74.3 %shard_map.77.both_ref = bf16[128,256]{1,0:T(8,128)(2,1)} custom-call(bf16[8,1024]{1,0:T(8,128)(2,1)} %bitcast.7, bf16[512,1024]{1,0:T(8,128)(2,1)} %inv_ref.1, s32[4,16]{1,0:T(4,128)} %map_ref.1, bf16[16,96,256]{2,1,0:T(8,128)(2,1)} %bitcast.5, bf16[2,768,256]{2,1,0:T(8,128)(2,1)} %bitcast.6, bf16[8,2,96,768]{3,2,1,0:T(8,128)(2,1)} %bitcast.4), custom_call_target="tpu_custom_call" | custom-call | tf_op jit(solution)/shard_map/pallas_call | solution.py:402
  74.9 1.5 %shard_map.78 = (bf16[32,256]{1,0:T(8,128)(2,1)}, bf16[1,96,256]{2,1,0:T(8,128)(2,1)}) custom-call(bf16[128,256]{1,0:T(8,128)(2,1)} %shard_map.77.both_ref), custom_call_target="tpu_custom_call" | custom-call | tf_op jit(solution)/shard_map/pallas_call | solution.py:421

commit v5 on v4

--- a/solution.py
+++ b/solution.py
@@ -125,7 +125,7 @@
         pltpu.make_async_copy(y_ref, k.y_v, k.load.at[5]),
         pltpu.make_async_copy(map_ref, k.map_v, k.load.at[6]),
     ]
-    for load in small + loads:
+    for load in small:
         load.start()
 
     barrier = pltpu.get_barrier_semaphore()
@@ -145,6 +145,8 @@
         for p in range(1, CHIP):
             greet((leaf, chip, 2 * ((chip + p) % CHIP) + core))
 
+    for load in loads:
+        load.start()
     small[0].wait()
     y = k.y_v[...].astype(F32)
     for part, at in ((k.ya, 0), (k.yb, 512)):
@@ -386,11 +388,13 @@
         both_ref[32:, h * W : (h + 1) * W] = gathered(h, k.cown, k.cin, k.crx).astype(BF)
 
     root_mm()
-    stages = [root_sum, y_spread, col_spread, panel_mm, panel_rs, panel_sum, child_mm, child_rs, child_sum]
-    for stage in stages:
+    groups = [(root_sum,), (y_spread,), (col_spread,), (panel_mm,), (panel_rs,), (panel_sum,), (child_mm, child_rs), (child_sum,)]
+    for group in groups:
         for h in range(NH):
-            stage(h)
-            if stage is panel_sum:
+            for stage in group:
+                stage(h)
+        if panel_sum in group:
+            for h in range(NH):
                 root_finish(h)
     for copy in sent:
         copy.wait_send()

time: 76.6 us -> 76.3 us (level)
  no operation moved by 1% of the time
where the time goes in v5:
time: 76.3 us; the launch traced here: 76.1 us
  Pallas kernels  75.4 us (99%)
    pallas_call x1, Pallas kernels, per_device(): pl.pallas_call(kernel, out_shape=jax.ShapeDtypeStruct((128, 256), BF), in...  74 us

profile of v5, /device:TPU:1, one launch (start us, length us, event | category | flops | bytes accessed | tf_op | source)
XLA Modules:
  0.0 76.1 jit_solution(7818035006153434870)
XLA Ops:
  0.6 74.0 %shard_map.77.both_ref = bf16[128,256]{1,0:T(8,128)(2,1)} custom-call(bf16[8,1024]{1,0:T(8,128)(2,1)} %bitcast.7, bf16[512,1024]{1,0:T(8,128)(2,1)} %inv_ref.1, s32[4,16]{1,0:T(4,128)} %map_ref.1, bf16[16,96,256]{2,1,0:T(8,128)(2,1)} %bitcast.5, bf16[2,768,256]{2,1,0:T(8,128)(2,1)} %bitcast.6, bf16[8,2,96,768]{3,2,1,0:T(8,128)(2,1)} %bitcast.4), custom_call_target="tpu_custom_call" | custom-call | tf_op jit(solution)/shard_map/pallas_call | solution.py:406
  74.6 1.5 %shard_map.78 = (bf16[32,256]{1,0:T(8,128)(2,1)}, bf16[1,96,256]{2,1,0:T(8,128)(2,1)}) custom-call(bf16[128,256]{1,0:T(8,128)(2,1)} %shard_map.77.both_ref), custom_call_target="tpu_custom_call" | custom-call | tf_op jit(solution)/shard_map/pallas_call | solution.py:425
